TPU v7x, 32 devices: a whole 2x2x4 slice. The times are simulated.
32 devices in a mesh: ctx: 8 (over z, y), head: 4 (over x, core).
Axes of the slice: x: 2, y: 2, z: 4, core: 2. Of those that a mesh axis runs over, the one named last changes fastest.
Arguments:
- queries: bfloat16 [4032, 4096], P('ctx', 'head'), may hold values from -6 to 6
- keys: bfloat16 [4032, 4096], P('ctx', 'head'), may hold values from -6 to 6
- values: bfloat16 [4032, 4096], P('ctx', 'head'), may hold values from -6 to 6
- out_weight: bfloat16 [4096, 4096], P('head'), may hold values from -0.09375 to 0.09375
- norm_gain: float32 [4096], P('head'), may hold values from 0.1 to 1.9
- tile_counts: int32 [8], replicated, may hold values from 1 to 63, as said below
- route_device: int32 [504], P('ctx'), may hold values from -1 to 7, as said below
- route_slot: int32 [504], P('ctx'), may hold values from -1 to 31, as said below
- session_starts: int32 [4], replicated, may hold values from 0 to 2047, as said below
Outputs:
- balanced_out: bfloat16 [2048, 4096], P('ctx', 'head')
Inputs may be any that keep to these rules, and one draw needn't show every extreme that they name: `tile_counts`: each value is at least 1 and the values sum to 256; some index has exactly 63 live tiles. `route_device`: the live tiles of an index are its first tile_counts slots; dead slots hold -1; each index of ctx receives exactly 32 tiles, and no index sends more than 8 tiles to one index. `route_slot`: dead slots hold -1; every pair of receiving index and slot below 32 is named by exactly one live tile. `session_starts`: strictly increasing, first value 0, last value 2048 - 1.
All inputs are finite; a program needn't handle non-finite values.
Results may differ from a plain program's by a relative error of at most 0.018.
Values may be sent and summed in bfloat16 or wider, within the bound.
A program may use at most 128 MiB of HBM per device.

v0:
```python
import jax
import jax.numpy as jnp
from jax import lax
from jax.sharding import PartitionSpec as P

DH = 128
CH = 8
BAL = 32


EPSILON = 1e-06


def carried_in(x, axis, combine, identity):
    count, here = (lax.axis_size(axis), lax.axis_index(axis))
    everything = jax.tree.map(
        lambda part, kind: lax.all_gather(part.astype(kind), axis), x, (jnp.bfloat16, jnp.bfloat16)
    )
    start = jax.tree.map(
        lambda part, zero: jnp.broadcast_to(jnp.asarray(zero, part.dtype), part.shape), x, identity
    )

    def step(k, before):
        reached = k < here
        new = combine(
            before, jax.tree.map(lambda part, own: part[k].astype(own.dtype), everything, x)
        )
        return jax.tree.map(lambda a, b: jnp.where(reached, a, b), new, before)

    return lax.fori_loop(0, count, step, start)


def feature(block):
    value = block.astype(jnp.float32)
    return jnp.where(value > 0, value + 1.0, jnp.exp(jnp.minimum(value, 0.0))).astype(jnp.bfloat16)


def split_parts(matrix):
    upper = matrix.astype(jnp.bfloat16)
    lower = (matrix - upper.astype(jnp.float32)).astype(jnp.bfloat16)
    return (upper, lower)


def session_of(session_starts, position):
    return jnp.sum((session_starts[None, :] <= position[:, None]).astype(jnp.int32), axis=1) - 1


def combine_states(earlier, later):
    return (jnp.maximum(earlier[0], later[0]), later[1] + (1.0 - later[0]) * earlier[1])


def deliver(payload, route_device, route_slot, ctx_size):
    slot_count = route_device.shape[0]
    columns = payload.shape[1]
    capacity = (slot_count + ctx_size - 1) // ctx_size
    tile_rows = payload.reshape(slot_count, CH * columns)
    ordinal = jnp.arange(slot_count)
    clashes = (route_device[None, :] == route_device[:, None]) & (
        ordinal[None, :] < ordinal[:, None]
    )
    before = jnp.sum(clashes.astype(jnp.int32), axis=1)
    target = jnp.where(route_device >= 0, route_device * capacity + before, -1)
    buckets = jnp.arange(ctx_size * capacity)
    chosen = buckets[:, None] == target[None, :]
    outgoing = jnp.dot(
        chosen.astype(jnp.bfloat16), tile_rows, preferred_element_type=jnp.float32
    ).astype(jnp.bfloat16)
    labels = jnp.sum(jnp.where(chosen, route_slot[None, :] + 1, 0), axis=1) - 1
    arrived, arrived_labels = (
        lax.all_to_all(outgoing, "ctx", split_axis=0, concat_axis=0, tiled=True),
        lax.all_to_all(labels, "ctx", split_axis=0, concat_axis=0, tiled=True),
    )
    wanted = jnp.arange(BAL)[:, None] == arrived_labels[None, :]
    placed = jnp.dot(
        wanted.astype(jnp.bfloat16), arrived, preferred_element_type=jnp.float32
    ).astype(jnp.bfloat16)
    return placed.reshape(BAL * CH, columns)


def per_device(
    queries,
    keys,
    values,
    out_weight,
    norm_gain,
    tile_counts,
    route_device,
    route_slot,
    session_starts,
):
    ctx_size = lax.axis_size("ctx")
    my_rank = lax.axis_index("ctx")
    slot_count = route_device.shape[0]
    row_count = slot_count * CH
    feature_width = queries.shape[1]
    head_count = feature_width // DH
    rank_ids = jnp.arange(ctx_size, dtype=jnp.int32)
    offset = CH * jnp.sum(jnp.where(rank_ids < my_rank, tile_counts, 0))
    my_count = jnp.sum(jnp.where(rank_ids == my_rank, tile_counts, 0))
    local_rows = jnp.arange(row_count, dtype=jnp.int32)
    is_live = local_rows // CH < my_count
    session = session_of(session_starts, offset + local_rows)
    prev_sess = session_of(session_starts, jnp.reshape(offset - 1, (1,)))[0]
    last_sess = session_of(session_starts, jnp.reshape(offset + my_count * CH - 1, (1,)))[0]
    query_feature_map = feature(queries).reshape(row_count, head_count, DH)
    key_map = feature(keys).reshape(row_count, head_count, DH)
    value_row_block = values.reshape(row_count, head_count, DH)
    key_mask = (is_live & (session == last_sess)).astype(jnp.bfloat16)
    masked_scores = key_map * key_mask[:, None, None]
    entry_value = jnp.einsum(
        "pld,plw->ldw", masked_scores, value_row_block, preferred_element_type=jnp.float32
    )
    reset_flag = (last_sess != prev_sess).astype(jnp.float32)
    carried = carried_in(
        (reset_flag, entry_value),
        "ctx",
        combine_states,
        (jnp.zeros((), jnp.float32), jnp.zeros_like(entry_value)),
    )
    incoming = carried[1]
    scores = jnp.einsum(
        "thd,shd->hts", query_feature_map, key_map, preferred_element_type=jnp.float32
    )
    allowed = (
        (local_rows[None, :] <= local_rows[:, None])
        & (session[None, :] == session[:, None])
        & is_live[None, :]
    )
    scores = jnp.where(allowed[None], scores, 0.0)
    score_upper, score_lower = split_parts(scores)
    inside = jnp.einsum(
        "hts,shd->thd", score_upper, value_row_block, preferred_element_type=jnp.float32
    )
    inside = inside + jnp.einsum(
        "hts,shd->thd", score_lower, value_row_block, preferred_element_type=jnp.float32
    )
    upper_state_half, lower_state_half = split_parts(incoming)
    carried_portion = jnp.einsum(
        "ycu,cux->ycx", query_feature_map, upper_state_half, preferred_element_type=jnp.float32
    )
    carried_portion = carried_portion + jnp.einsum(
        "ycu,cux->ycx", query_feature_map, lower_state_half, preferred_element_type=jnp.float32
    )
    carried_portion = jnp.where((session == prev_sess)[:, None, None], carried_portion, 0.0)
    numerator = inside + carried_portion
    inverse_rms = lax.rsqrt(jnp.mean(numerator * numerator, axis=-1, keepdims=True) + EPSILON)
    attended = (
        (numerator * inverse_rms * norm_gain.reshape(head_count, DH))
        .astype(jnp.bfloat16)
        .reshape(row_count, feature_width)
    )
    partial_value = jnp.dot(attended, out_weight, preferred_element_type=jnp.float32)
    payload = lax.psum_scatter(
        partial_value.astype(jnp.bfloat16), "head", scatter_dimension=1, tiled=True
    )
    delivered = deliver(payload, route_device, route_slot, ctx_size)
    return delivered


def solution(mesh):
    placed = (
        P("ctx", "head"),
        P("ctx", "head"),
        P("ctx", "head"),
        P("head", None),
        P("head"),
        P(),
        P("ctx"),
        P("ctx"),
        P(),
    )
    return jax.shard_map(
        per_device, mesh=mesh, in_specs=placed, out_specs=P("ctx", "head"), check_vma=False
    )
```

profile of v0, /device:TPU:0, one launch (start us, length us, event | category | flops | bytes accessed | tf_op | source)
XLA Modules:
  0.0 189.2 jit_solution(12494763034591143721)
XLA Ops:
  6.5 1.4 fusion.47
  9.2 1.4 fusion.48
  11.9 0.7 convert_reduce_fusion.1
  13.3 2.9 %convolution_convert_fusion.3 = bf16[8,128,128]{2,1,0:T(8,128)(2,1)} fusion(bf16[504]{0:T(512)(128)(2,1)S(1)} %get-tuple-element.133, bf16[504,1024]{1,0:T(8,128)(2,1)S(1)} %copy-done, bf16[504,1024]{1,0:T(8,128)(2,1)} %param.12), kind=kOutput, calls=%fused_computation.29 | convolution fusion | flops 137412608 | bytes 2327536 | tf_op jit(solution)/shard_map/pld,plw->ldw/dot_general | solution.py:110
  17.0 0.7 dynamic-update-slice
  17.7 23.2 %all-reduce = bf16[8]{0:T(256)(128)(2,1)S(1)} all-reduce(bf16[8]{0:T(256)(128)(2,1)S(1)} %dynamic-update-slice), channel_id=1, replica_groups=mesh['ctx'=8,'head'=4] {'ctx'}, use_global_device_ids=true, to_apply=%add | all-reduce | flops 8 | bytes 32
  41.7 2.5 %fusion.20 = f32[8,504,504]{2,1,0:T(8,128)S(1)} fusion(bf16[504,1024]{1,0:T(8,128)(2,1)} %param.12, bf16[504,1024]{1,0:T(8,128)(2,1)S(1)} %copy-done.2), kind=kOutput, calls=%fused_computation.37 | convolution fusion | flops 526417920 | bytes 10192896 | tf_op jit(solution)/shard_map/thd,shd->hts/dot_general | solution.py:121
  44.3 2.6 %fusion.2 = f32[8,504,128]{2,1,0:T(8,128)} fusion(f32[8,504,504]{2,1,0:T(8,128)S(1)} %fusion.20, pred[504,504]{1,0:T(8,128)(4,1)S(1)} %fusion.27, bf16[504,1024]{1,0:T(8,128)(2,1)S(1)} %copy-done), kind=kOutput, calls=%fused_computation.8 | convolution fusion | flops 522256896 | bytes 11479104 | tf_op jit(solution)/shard_map/hts,shd->thd/dot_general | solution.py:131
  46.9 2.7 %fusion.3 = f32[8,504,128]{2,1,0:T(8,128)} fusion(f32[8,504,504]{2,1,0:T(8,128)S(1)} %fusion.20, pred[504,504]{1,0:T(8,128)(4,1)S(1)} %fusion.27, bf16[504,1024]{1,0:T(8,128)(2,1)S(1)} %copy-done), kind=kOutput, calls=%fused_computation.9 | convolution fusion | flops 530385408 | bytes 11479104 | tf_op jit(solution)/shard_map/hts,shd->thd/dot_general | solution.py:134
  49.7 18.8 %all-gather.3.cloned.1.call-done = bf16[64,128,128]{2,1,0:T(8,128)(2,1)} async-done(((bf16[8,128,128]{2,1,0:T(8,128)(2,1)}), bf16[64,128,128]{2,1,0:T(8,128)(2,1)}) %all-gather.3.cloned.1.call-update) | async-done | bytes 2097168 | tf_op jit(solution)/shard_map/all_gather | solution.py:17
  68.5 20.4 %while.14 = (s32[]{:T(128)}, f32[8,128,128]{2,1,0:T(8,128)S(1)}, s32[]{:T(128)}, bf16[8,8,128,128]{3,2,1,0:T(8,128)(2,1)}, bf16[8]{0:T(256)(128)(2,1)S(1)}, /*index=5*/s32[]{:T(128)}, f32[1]{0:T(128)}, s32[]{:T(128)}) while((s32[]{:T(128)}, f32[8,128,128]{2,1,0:T(8,128)S(1)}, s32[]{:T(128)}, bf16[8,8,128,128]{3,2,1,0:T(8,128)(2,1)}, ...), condition=%wide.region_8.9_spmd.clone, body=%wide.region_7.8_spmd.clone.sunk | while | flops 655365 | bytes 1310851 | solution.py:30
  69.8 1.3 fusion.69
  72.3 1.3 fusion.69
  74.9 1.3 fusion.69
  77.4 1.3 fusion.69
  80.0 1.3 fusion.69
  82.5 1.3 fusion.69
  85.1 1.3 fusion.69
  87.6 1.3 fusion.69
  88.9 0.7 fusion.23
  89.6 0.9 copy-done.1
  90.5 2.8 %multiply_reduce_fusion = (f32[504,8]{0,1:T(8,128)S(1)}, f32[504,8,128]{2,0,1:T(8,128)S(1)}) fusion(f32[8,128,504]{1,2,0:T(8,128)S(1)} %fusion.23, f32[8,128,128]{2,1,0:T(8,128)S(1)} %get-tuple-element.99, pred[504]{0:T(512)(128)(4,1)S(1)} %get-tuple-element.132, f32[8,504,128]{2,1,0:T(8,128)S(1)} %copy-done.1, f32[8,504,128]{2,1,0:T(8,128)} %fusion.3, ...), kind=kOutput, calls=%fused_computation.28 | convolution fusion | flops 138833984 | bytes 9830648 | tf_op jit(solution)/shard_map/ycu,cux->ycx/dot_general | solution.py:141
  93.3 0.7 multiply_convert_fusion
  94.6 9.5 %convolution_convert_fusion.2 = bf16[504,4096]{1,0:T(8,128)(2,1)} fusion(bf16[504,1024]{0,1:T(8,128)(2,1)S(1)} %bitcast.72, bf16[1024,4096]{1,0:T(8,128)(2,1)} %param.14), kind=kOutput, calls=%fused_computation.7 | convolution fusion | flops 4229922816 | bytes 13549568 | tf_op jit(solution)/shard_map/dot_general | solution.py:152
  105.0 0.7 sub.45
  105.7 3.3 %all-to-all-start = ((s32[8,8,1]{1,2,0:T(1,128)}), s32[8,8,1]{1,2,0:T(1,128)S(1)}, u32[]{:S(2)}, u32[]{:S(2)}) async-start(s32[8,8,1]{1,2,0:T(1,128)} %bitcast), calls=%async_computation | async-start | bytes 8192 | tf_op jit(solution)/shard_map/all_to_all | solution.py:71
  109.0 37.8 %reduce-scatter.2.cloned.1.call-done = bf16[504,1024]{1,0:T(8,128)(2,1)} async-done(((bf16[504,4096]{1,0:T(8,128)(2,1)}), bf16[504,1024]{1,0:T(8,128)(2,1)}) %reduce-scatter.2.cloned.1.call-update) | async-done | bytes 1032208 | tf_op jit(solution)/shard_map/reduce_scatter | solution.py:153
  146.8 1.6 reshape.180
  148.4 1.4 fusion.1
  149.8 5.5 %all-to-all-start.1 = ((bf16[8,8,8192]{2,1,0:T(8,128)(2,1)}), bf16[8,8,8192]{2,1,0:T(8,128)(2,1)S(1)}, u32[]{:S(2)}, u32[]{:S(2)}) async-start(bf16[8,8,8192]{2,1,0:T(8,128)(2,1)} %fusion.1), calls=%async_computation.2 | async-start | bytes 2097152 | tf_op jit(solution)/shard_map/all_to_all | solution.py:70
  156.6 24.5 %all-to-all-done.1 = bf16[8,8,8192]{2,1,0:T(8,128)(2,1)S(1)} async-done(((bf16[8,8,8192]{2,1,0:T(8,128)(2,1)}), bf16[8,8,8192]{2,1,0:T(8,128)(2,1)S(1)}, u32[]{:S(2)}, u32[]{:S(2)}) %all-to-all-start.1) | async-done | bytes 1048608 | tf_op jit(solution)/shard_map/all_to_all | solution.py:70
  181.4 1.0 reshape.181
  (45 shorter events, 9.9 us)
Async XLA Ops:
  6.5 6.8 %copy-start = (bf16[504,1024]{1,0:T(8,128)(2,1)S(1)}, bf16[504,1024]{1,0:T(8,128)(2,1)}, u32[]{:S(2)}) copy-start(bf16[504,1024]{1,0:T(8,128)(2,1)} %param.13) | copy-start | bytes 3096580
  6.5 62.0 %all-gather.3.cloned.1.call-start = ((), (), s32[]{:S(2)}) async-start(), calls=%async_computation.4 | async-start | bytes 2359296 | tf_op jit(solution)/shard_map/all_gather | solution.py:17
  13.3 3.0 %copy-start.6 = (u32[32]{0:T(128)S(1)}, u32[32]{0:T(128)}, u32[]{:S(2)}) copy-start(u32[32]{0:T(128)} %constant.88) | copy-start | bytes 388
  13.3 28.4 %copy-start.2 = (bf16[504,1024]{1,0:T(8,128)(2,1)S(1)}, bf16[504,1024]{1,0:T(8,128)(2,1)}, u32[]{:S(2)}) copy-start(bf16[504,1024]{1,0:T(8,128)(2,1)} %param.11) | copy-start | bytes 3096580
  16.3 130.5 %reduce-scatter.2.cloned.1.call-start = ((), (), s32[]{:S(2)}) async-start(), calls=%async_computation.3 | async-start | bytes 5160960 | tf_op jit(solution)/shard_map/reduce_scatter | solution.py:153
  88.9 1.6 copy-start.1
  90.5 2.8 %copy-start.3 = (f32[1024]{0:T(1024)S(1)}, f32[1024]{0:T(1024)}, u32[]{:S(2)}) copy-start(f32[1024]{0:T(1024)} %param.15) | copy-start | bytes 12292
  104.0 0.7 copy-start.5
  104.0 0.8 copy-start.4
  105.7 44.1 %all-to-all-start = ((s32[8,8,1]{1,2,0:T(1,128)}), s32[8,8,1]{1,2,0:T(1,128)S(1)}, u32[]{:S(2)}, u32[]{:S(2)}) async-start(s32[8,8,1]{1,2,0:T(1,128)} %bitcast), calls=%async_computation | async-start | bytes 8192 | tf_op jit(solution)/shard_map/all_to_all | solution.py:71
  149.8 31.3 %all-to-all-start.1 = ((bf16[8,8,8192]{2,1,0:T(8,128)(2,1)}), bf16[8,8,8192]{2,1,0:T(8,128)(2,1)S(1)}, u32[]{:S(2)}, u32[]{:S(2)}) async-start(bf16[8,8,8192]{2,1,0:T(8,128)(2,1)} %fusion.1), calls=%async_computation.2 | async-start | bytes 2097152 | tf_op jit(solution)/shard_map/all_to_all | solution.py:70
Sparse Core Ops, SparseCore 0:
  16.4 52.0 all-gather.2
  104.2 42.5 reduce-scatter.1
where the time goes:
time: 190 us; the launch traced here: 189 us
  waiting for transfers between devices  81.2 us (43%)
  matrix products  25.5 us (13%)
  blocking collectives  23.2 us (12%)
  other arithmetic  16.9 us (9%)
  between operations  16.2 us (9%)
  local copies, waits for them, and re-layouts  11.9 us (6%)
  starting transfers between devices  8.88 us (5%)
  loops' own time  5.41 us (3%)
    reduce_scatter x1, waiting for transfers between devices, per_device(): lax.psum_scatter(partial_value.astype(jnp.bfloat16), 'head', scatter_dime...  37.8 us
    all_to_all x1, waiting for transfers between devices, deliver(): lax.all_to_all(outgoing, 'ctx', split_axis=0, concat_axis=0, tiled=True)  24.5 us
    unnamed x1, blocking collectives  23.2 us
    all_gather x1, waiting for transfers between devices, carried_in(): lax.all_gather(part.astype(kind), axis)  18.8 us
    select_n x8, other arithmetic, step(): return jax.tree.map(lambda a, b: jnp.where(reached, a, b), new, before)  10.3 us
    dot_general x1, matrix products, per_device(): jnp.dot(attended, out_weight, preferred_element_type=jnp.float32)  9.47 us
    all_to_all x1, starting transfers between devices, deliver(): lax.all_to_all(outgoing, 'ctx', split_axis=0, concat_axis=0, tiled=True)  5.51 us
    another operation x1, loops' own time, carried_in(): return lax.fori_loop(0, count, step, start)  5.41 us
  transfers between devices with their start and end apart: 4, of which 3 were waited for; matrix products, arithmetic and copies ran while one was open for 8% of the time, Pallas kernels for 0%

commit v1 on v0

--- a/solution.py
+++ b/solution.py
@@ -149,12 +149,11 @@
         .astype(jnp.bfloat16)
         .reshape(row_count, feature_width)
     )
-    partial_value = jnp.dot(attended, out_weight, preferred_element_type=jnp.float32)
-    payload = lax.psum_scatter(
+    delivered = deliver(attended, route_device, route_slot, ctx_size)
+    partial_value = jnp.dot(delivered, out_weight, preferred_element_type=jnp.float32)
+    return lax.psum_scatter(
         partial_value.astype(jnp.bfloat16), "head", scatter_dimension=1, tiled=True
     )
-    delivered = deliver(payload, route_device, route_slot, ctx_size)
-    return delivered
 
 
 def solution(mesh):

time: 190 us -> 171 us (0.900)
  waiting for transfers between devices: 81.2 us -> 66 us
  local copies, waits for them, and re-layouts: 11.9 us -> 9.1 us
  starting transfers between devices: 8.88 us -> 11.1 us
  matrix products: 25.5 us -> 23.5 us
    reduce_scatter x1, waiting for transfers between devices: 37.8 us -> 30.4 us  [per_device(): lax.psum_scatter(partial_value.astype(jnp.bfloat16), 'head', scatter_dime...]
    all_gather x1, waiting for transfers between devices: 18.8 us -> 11.6 us  [carried_in(): lax.all_gather(part.astype(kind), axis)]
    all_to_all x1, starting transfers between devices: 3.33 us -> 7.28 us  [deliver(): lax.all_to_all(labels, 'ctx', split_axis=0, concat_axis=0, tiled=True)]
    dot_general x1, matrix products: 9.47 us -> 7.11 us  [per_device(): jnp.dot(delivered, out_weight, preferred_element_type=jnp.float32)]
    all_to_all x1, starting transfers between devices: 5.51 us -> 3.56 us  [deliver(): lax.all_to_all(outgoing, 'ctx', split_axis=0, concat_axis=0, tiled=True)]
  transfers between devices with their start and end apart: 4 -> 4, of which waited for: 3 -> 3; matrix products, arithmetic and copies ran while one was open for 8% -> 20% of each run, Pallas kernels for 0% -> 0%
where the time goes in v1:
time: 171 us; the launch traced here: 170 us
  waiting for transfers between devices  66 us (39%)
  matrix products  23.5 us (14%)
  blocking collectives  22 us (13%)
  other arithmetic  16.9 us (10%)
  between operations  16.2 us (9%)
  starting transfers between devices  11.1 us (6%)
  local copies, waits for them, and re-layouts  9.1 us (5%)
  loops' own time  5.41 us (3%)
    reduce_scatter x1, waiting for transfers between devices, per_device(): lax.psum_scatter(partial_value.astype(jnp.bfloat16), 'head', scatter_dime...  30.4 us
    all_to_all x1, waiting for transfers between devices, deliver(): lax.all_to_all(outgoing, 'ctx', split_axis=0, concat_axis=0, tiled=True)  24 us
    unnamed x1, blocking collectives  22 us
    all_gather x1, waiting for transfers between devices, carried_in(): lax.all_gather(part.astype(kind), axis)  11.6 us
    select_n x8, other arithmetic, step(): return jax.tree.map(lambda a, b: jnp.where(reached, a, b), new, before)  10.3 us
    all_to_all x1, starting transfers between devices, deliver(): lax.all_to_all(labels, 'ctx', split_axis=0, concat_axis=0, tiled=True)  7.28 us
    dot_general x1, matrix products, per_device(): jnp.dot(delivered, out_weight, preferred_element_type=jnp.float32)  7.11 us
    another operation x1, loops' own time, carried_in(): return lax.fori_loop(0, count, step, start)  5.41 us
  transfers between devices with their start and end apart: 4, of which 3 were waited for; matrix products, arithmetic and copies ran while one was open for 20% of the time, Pallas kernels for 0%

profile of v1, /device:TPU:0, one launch (start us, length us, event | category | flops | bytes accessed | tf_op | source)
XLA Modules:
  0.0 170.2 jit_solution(5630941740345217843)
XLA Ops:
  6.5 1.4 fusion.47
  9.2 1.4 fusion.48
  11.9 0.7 convert_reduce_fusion.1
  13.4 2.9 %convolution_convert_fusion.3 = bf16[8,128,128]{2,1,0:T(8,128)(2,1)} fusion(bf16[504]{0:T(512)(128)(2,1)S(1)} %get-tuple-element.133, bf16[504,1024]{1,0:T(8,128)(2,1)S(1)} %copy-done, bf16[504,1024]{1,0:T(8,128)(2,1)} %param.12), kind=kOutput, calls=%fused_computation.29 | convolution fusion | flops 137412608 | bytes 2327536 | tf_op jit(solution)/shard_map/pld,plw->ldw/dot_general | solution.py:110
  16.7 0.7 sub.45
  17.9 0.7 dynamic-update-slice
  18.7 7.3 %all-to-all-start = ((s32[8,8,1]{1,2,0:T(1,128)}), s32[8,8,1]{1,2,0:T(1,128)S(1)}, u32[]{:S(2)}, u32[]{:S(2)}) async-start(s32[8,8,1]{1,2,0:T(1,128)} %bitcast), calls=%async_computation | async-start | bytes 8192 | tf_op jit(solution)/shard_map/all_to_all | solution.py:71
  25.9 22.0 %all-reduce = bf16[8]{0:T(256)(128)(2,1)S(1)} all-reduce(bf16[8]{0:T(256)(128)(2,1)S(1)} %dynamic-update-slice), channel_id=1, replica_groups=mesh['ctx'=8,'head'=4] {'ctx'}, use_global_device_ids=true, to_apply=%add | all-reduce | flops 8 | bytes 32
  47.9 0.6 fusion.42
  48.8 2.5 %fusion.20 = f32[8,504,504]{2,1,0:T(8,128)S(1)} fusion(bf16[504,1024]{1,0:T(8,128)(2,1)} %param.12, bf16[504,1024]{1,0:T(8,128)(2,1)S(1)} %copy-done.2), kind=kOutput, calls=%fused_computation.37 | convolution fusion | flops 526417920 | bytes 10192896 | tf_op jit(solution)/shard_map/thd,shd->hts/dot_general | solution.py:121
  51.3 2.9 %fusion.2 = f32[8,504,128]{2,1,0:T(8,128)} fusion(f32[8,504,504]{2,1,0:T(8,128)S(1)} %fusion.20, pred[504,504]{1,0:T(8,128)(4,1)S(1)} %fusion.27, bf16[504,1024]{1,0:T(8,128)(2,1)S(1)} %copy-done), kind=kOutput, calls=%fused_computation.7 | convolution fusion | flops 522256896 | bytes 11479104 | tf_op jit(solution)/shard_map/hts,shd->thd/dot_general | solution.py:131
  54.2 2.9 %fusion.3 = f32[8,504,128]{2,1,0:T(8,128)} fusion(f32[8,504,504]{2,1,0:T(8,128)S(1)} %fusion.20, pred[504,504]{1,0:T(8,128)(4,1)S(1)} %fusion.27, bf16[504,1024]{1,0:T(8,128)(2,1)S(1)} %copy-done), kind=kOutput, calls=%fused_computation.9 | convolution fusion | flops 530385408 | bytes 11479104 | tf_op jit(solution)/shard_map/hts,shd->thd/dot_general | solution.py:134
  57.1 11.6 %all-gather.3.cloned.1.call-done = bf16[64,128,128]{2,1,0:T(8,128)(2,1)} async-done(((bf16[8,128,128]{2,1,0:T(8,128)(2,1)}), bf16[64,128,128]{2,1,0:T(8,128)(2,1)}) %all-gather.3.cloned.1.call-update) | async-done | bytes 2097168 | tf_op jit(solution)/shard_map/all_gather | solution.py:17
  68.7 20.4 %while.14 = (s32[]{:T(128)}, f32[8,128,128]{2,1,0:T(8,128)S(1)}, s32[]{:T(128)}, bf16[8,8,128,128]{3,2,1,0:T(8,128)(2,1)}, bf16[8]{0:T(256)(128)(2,1)S(1)}, /*index=5*/s32[]{:T(128)}, f32[1]{0:T(128)}, s32[]{:T(128)}) while((s32[]{:T(128)}, f32[8,128,128]{2,1,0:T(8,128)S(1)}, s32[]{:T(128)}, bf16[8,8,128,128]{3,2,1,0:T(8,128)(2,1)}, ...), condition=%wide.region_8.9_spmd.clone, body=%wide.region_7.8_spmd.clone.sunk | while | flops 655365 | bytes 1310851 | solution.py:30
  70.0 1.3 fusion.69
  72.5 1.3 fusion.69
  75.0 1.3 fusion.69
  77.6 1.3 fusion.69
  80.1 1.3 fusion.69
  82.7 1.3 fusion.69
  85.2 1.3 fusion.69
  87.8 1.3 fusion.69
  89.1 0.7 fusion.23
  89.8 0.9 copy-done.1
  90.7 2.8 %multiply_reduce_fusion = (f32[504,8]{0,1:T(8,128)S(1)}, f32[504,8,128]{2,0,1:T(8,128)S(1)}) fusion(f32[8,128,504]{1,2,0:T(8,128)S(1)} %fusion.23, f32[8,128,128]{2,1,0:T(8,128)S(1)} %get-tuple-element.99, pred[504]{0:T(512)(128)(4,1)S(1)} %get-tuple-element.132, f32[8,504,128]{2,1,0:T(8,128)S(1)} %copy-done.1, f32[8,504,128]{2,1,0:T(8,128)} %fusion.3, ...), kind=kOutput, calls=%fused_computation.28 | convolution fusion | flops 138833984 | bytes 9830648 | tf_op jit(solution)/shard_map/ycu,cux->ycx/dot_general | solution.py:141
  93.5 0.7 multiply_convert_fusion
  94.9 1.4 fusion.1
  96.3 3.6 %all-to-all-start.1 = ((bf16[8,8,8192]{2,1,0:T(8,128)(2,1)}), bf16[8,8,8192]{2,1,0:T(8,128)(2,1)S(1)}, u32[]{:S(2)}, u32[]{:S(2)}) async-start(bf16[8,8,8192]{2,1,0:T(8,128)(2,1)} %fusion.1), calls=%async_computation.1 | async-start | bytes 2097152 | tf_op jit(solution)/shard_map/all_to_all | solution.py:70
  100.6 0.7 reduce.7
  101.3 24.0 %all-to-all-done.1 = bf16[8,8,8192]{2,1,0:T(8,128)(2,1)S(1)} async-done(((bf16[8,8,8192]{2,1,0:T(8,128)(2,1)}), bf16[8,8,8192]{2,1,0:T(8,128)(2,1)S(1)}, u32[]{:S(2)}, u32[]{:S(2)}) %all-to-all-start.1) | async-done | bytes 1048608 | tf_op jit(solution)/shard_map/all_to_all | solution.py:70
  125.8 7.1 %convolution_convert_fusion.2 = bf16[256,4096]{1,0:T(8,128)(2,1)} fusion(bf16[256,1024]{1,0:T(8,128)(2,1)S(1)} %reshape.173, bf16[1024,4096]{1,0:T(8,128)(2,1)} %param.14), kind=kOutput, calls=%fused_computation.8 | convolution fusion | flops 2148532224 | bytes 11010048 | tf_op jit(solution)/shard_map/dot_general | solution.py:153
  133.0 30.4 %reduce-scatter.2.cloned.1.call-done = bf16[256,1024]{1,0:T(8,128)(2,1)} async-done(((bf16[256,4096]{1,0:T(8,128)(2,1)}), bf16[256,1024]{1,0:T(8,128)(2,1)}) %reduce-scatter.2.cloned.1.call-update) | async-done | bytes 524304 | tf_op jit(solution)/shard_map/reduce_scatter | solution.py:154
  (44 shorter events, 8.5 us)
Async XLA Ops:
  6.5 6.8 %copy-start = (bf16[504,1024]{1,0:T(8,128)(2,1)S(1)}, bf16[504,1024]{1,0:T(8,128)(2,1)}, u32[]{:S(2)}) copy-start(bf16[504,1024]{1,0:T(8,128)(2,1)} %param.13) | copy-start | bytes 3096580
  6.5 62.2 %all-gather.3.cloned.1.call-start = ((), (), s32[]{:S(2)}) async-start(), calls=%async_computation.4 | async-start | bytes 2359296 | tf_op jit(solution)/shard_map/all_gather | solution.py:17
  13.3 3.0 %copy-start.4 = (s32[63]{0:T(128)S(1)}, s32[63]{0:T(128)}, u32[]{:S(2)}) copy-start(s32[63]{0:T(128)} %param.17) | copy-start | bytes 760
  13.3 3.2 %copy-start.5 = (s32[63]{0:T(128)S(1)}, s32[63]{0:T(128)}, u32[]{:S(2)}) copy-start(s32[63]{0:T(128)} %param.18) | copy-start | bytes 760
  13.3 4.0 %copy-start.6 = (u32[32]{0:T(128)S(1)}, u32[32]{0:T(128)}, u32[]{:S(2)}) copy-start(u32[32]{0:T(128)} %constant.88) | copy-start | bytes 388
  13.3 35.4 %copy-start.2 = (bf16[504,1024]{1,0:T(8,128)(2,1)S(1)}, bf16[504,1024]{1,0:T(8,128)(2,1)}, u32[]{:S(2)}) copy-start(bf16[504,1024]{1,0:T(8,128)(2,1)} %param.11) | copy-start | bytes 3096580
  18.7 77.6 %all-to-all-start = ((s32[8,8,1]{1,2,0:T(1,128)}), s32[8,8,1]{1,2,0:T(1,128)S(1)}, u32[]{:S(2)}, u32[]{:S(2)}) async-start(s32[8,8,1]{1,2,0:T(1,128)} %bitcast), calls=%async_computation | async-start | bytes 8192 | tf_op jit(solution)/shard_map/all_to_all | solution.py:71
  89.1 1.6 copy-start.1
  90.7 2.8 %copy-start.3 = (f32[1024]{0:T(1024)S(1)}, f32[1024]{0:T(1024)}, u32[]{:S(2)}) copy-start(f32[1024]{0:T(1024)} %param.15) | copy-start | bytes 12292
  96.3 29.0 %all-to-all-start.1 = ((bf16[8,8,8192]{2,1,0:T(8,128)(2,1)}), bf16[8,8,8192]{2,1,0:T(8,128)(2,1)S(1)}, u32[]{:S(2)}, u32[]{:S(2)}) async-start(bf16[8,8,8192]{2,1,0:T(8,128)(2,1)} %fusion.1), calls=%async_computation.1 | async-start | bytes 2097152 | tf_op jit(solution)/shard_map/all_to_all | solution.py:70
  99.8 63.5 %reduce-scatter.2.cloned.1.call-start = ((), (), s32[]{:S(2)}) async-start(), calls=%async_computation.3 | async-start | bytes 2621440 | tf_op jit(solution)/shard_map/reduce_scatter | solution.py:154
Sparse Core Ops, SparseCore 0:
  16.4 52.2 all-gather.2
  133.1 30.2 reduce-scatter.1

commit v2 on v1

v2 whole, which is shorter than its diff:
```python
import functools

import jax
import jax.numpy as jnp
from jax import lax
from jax.experimental import pallas as pl
from jax.experimental.pallas import tpu as pltpu
from jax.sharding import PartitionSpec as P

DH = 128
CH = 8
BAL = 32


EPSILON = 1e-06


MESH = pl.DeviceIdType.MESH
STEP = 256


def offsets_far_first(n):
    order = sorted(range(1, n), key=lambda o: -min(o, n - o))
    return order


def greet(targets):
    barrier = pltpu.get_barrier_semaphore()
    for target in targets:
        pl.semaphore_signal(barrier, inc=1, device_id=target, device_id_type=MESH)
    pl.semaphore_wait(barrier, len(targets))


def feature(block):
    value = block.astype(jnp.float32)
    return jnp.where(value > 0, value + 1.0, jnp.exp(jnp.minimum(value, 0.0)))


def whole_kernel(
    n, groups, steps, parts, counts_ref, starts_ref, q_ref, k_ref, v_ref, gain_ref, target_ref, labels_ref, weight_ref, out_ref,
    kf, vf, mask, chosen, attended, own, sent, pair_in, chain_in, chain_out, got,
    buckets, arrived, total, weight, placed, s1, r1, s2, r2, s3, r3, keep,
    pair_send, pair_recv, chain_send, chain_recv, lab_send, lab_recv, lab_own,
    w_sem, a_send, a_recv, a_own, x1s, x1r, x2s, x2r, x3s, x3r,
):
    me = lax.axis_index("ctx")
    mine = lax.axis_index("head")
    a, b = mine // 2, mine % 2
    sib = 2 * a + 1 - b
    far = 2 * (1 - a) + b
    far_sib = 2 * (1 - a) + 1 - b
    pair, side = me // 2, me % 2
    partner = me + 1 - 2 * side
    has_prev = pair > 0
    has_next = pair < n // 2 - 1
    rows, features = q_ref.shape
    full = kf.shape[0]
    heads = features // DH
    span = features // parts
    order = offsets_far_first(n)
    width = steps * STEP
    targets = (far_sib, far, sib, mine)

    def load(i):
        return pltpu.make_async_copy(
            weight_ref.at[:, pl.ds(pl.multiple_of(targets[i] * width, width), width)], weight.at[i], w_sem.at[i]
        )

    def pair_copy(h):
        return pltpu.make_async_remote_copy(
            src_ref=sent.at[h], dst_ref=pair_in.at[h], send_sem=pair_send.at[h], recv_sem=pair_recv.at[h],
            device_id={"ctx": partner}, device_id_type=MESH,
        )

    def chain_copy(h):
        return pltpu.make_async_remote_copy(
            src_ref=chain_out.at[h], dst_ref=chain_in.at[h], send_sem=chain_send.at[h], recv_sem=chain_recv.at[h],
            device_id={"ctx": lax.rem(me + 2, n)}, device_id_type=MESH,
        )

    def label_copy(o):
        return pltpu.make_async_remote_copy(
            src_ref=labels_ref.at[lax.rem(me + o, n)], dst_ref=got.at[o], send_sem=lab_send.at[o],
            recv_sem=lab_recv.at[o], device_id={"ctx": lax.rem(me + o, n)}, device_id_type=MESH,
        )

    def tile_copy(g, o):
        to = lax.rem(me + o, n)
        return pltpu.make_async_remote_copy(
            src_ref=buckets.at[g, to], dst_ref=arrived.at[g, o], send_sem=a_send.at[g, o], recv_sem=a_recv.at[g, o],
            device_id={"ctx": to}, device_id_type=MESH,
        )

    def own_copy(g):
        return pltpu.make_async_copy(buckets.at[g, me], arrived.at[g, 0], a_own.at[g])

    def move(src, dst, send, recv, j, to):
        return pltpu.make_async_remote_copy(
            src_ref=src.at[j], dst_ref=dst.at[j], send_sem=send.at[j], recv_sem=recv.at[j],
            device_id={"head": to}, device_id_type=MESH,
        )

    for i in range(4):
        load(i).start()
    greet([{"ctx": lax.rem(me + o, n)} for o in range(1, n)] + [{"head": sib}, {"head": far}])

    counts = [counts_ref[i] for i in range(n)]

    def tiles_before(index):
        result = jnp.int32(0)
        for i in range(n):
            result = result + jnp.where(i < index, counts[i], 0)
        return result

    def session_at(position):
        result = jnp.zeros_like(position) - 1
        for i in range(starts_ref.shape[0]):
            result = result + jnp.where(starts_ref[i] <= position, 1, 0)
        return result

    def last_of(index):
        return session_at(CH * tiles_before(index + 1) - 1)

    def same(x, y):
        return jnp.where(x == y, jnp.float32(1.0), jnp.float32(0.0))

    offset = CH * tiles_before(me)
    live_end = CH * tiles_before(me + 1)
    last_sess, prev_sess = last_of(me), session_at(offset - 1)
    first, second = last_of(2 * pair), last_of(2 * pair + 1)
    before_pair = last_of(2 * pair - 1)
    joined = same(first, second)
    own_weight = jnp.where(side == 0, joined, 1.0)
    other_weight = jnp.where(side == 0, 1.0, joined)
    chain_weight = same(before_pair, second)
    inc_other = jnp.where(side == 0, 0.0, 1.0)
    inc_chain = jnp.where(side == 0, 1.0, same(before_pair, first))

    column = offset + lax.broadcasted_iota(jnp.int32, (full, DH), 0)
    column_sess = session_at(column)
    key_mask = jnp.where((column < live_end) & (column_sess == last_sess), 1.0, 0.0).astype(jnp.bfloat16)
    carry_mask = jnp.where(column_sess == prev_sess, 1.0, 0.0)

    def pad(block):
        return jnp.concatenate([block, jnp.zeros((full - rows, DH), jnp.float32)], axis=0)

    def columns_of(h):
        return pl.ds(pl.multiple_of(h * DH, DH), DH)

    def enter(h, _):
        cols = columns_of(h)
        key = pad(feature(k_ref[:, cols])).astype(jnp.bfloat16)
        value = pad(v_ref[:, cols].astype(jnp.float32)).astype(jnp.bfloat16)
        kf[:, cols] = key
        vf[:, cols] = value
        entry = lax.dot_general(
            key * key_mask, value, (((0,), (0,)), ((), ())), preferred_element_type=jnp.float32
        )
        own[h] = entry
        sent[h] = entry.astype(jnp.bfloat16)
        pair_copy(h).start()
        return 0

    lax.fori_loop(0, heads, enter, 0)

    for o in range(1, n):
        label_copy(o).start()
    label_own = pltpu.make_async_copy(labels_ref.at[me], got.at[0], lab_own)
    label_own.start()

    @pl.when(jnp.logical_not(has_prev))
    def _():
        chain_in[...] = jnp.zeros_like(chain_in)

    at_row = offset + lax.broadcasted_iota(jnp.int32, (full, full), 0)
    at_col = offset + lax.broadcasted_iota(jnp.int32, (full, full), 1)
    mask[...] = jnp.where(
        (at_col <= at_row) & (at_col < live_end) & (session_at(at_col) == session_at(at_row)), 1.0, 0.0
    ).astype(jnp.bfloat16)
    spots = buckets.shape[1] * buckets.shape[2]
    chosen[...] = jnp.where(
        lax.broadcasted_iota(jnp.int32, (spots, full), 0) == target_ref[...], 1.0, 0.0
    ).astype(jnp.bfloat16)
    half = full // 2

    def inner(h):
        cols = columns_of(h)
        query = pad(feature(q_ref[:, cols])).astype(jnp.bfloat16)

        def block(lo, hi):
            scores = lax.dot_general(
                query[lo:hi], kf[:hi, cols], (((1,), (1,)), ((), ())), preferred_element_type=jnp.float32
            )
            return jnp.dot(
                scores.astype(jnp.bfloat16) * mask[lo:hi, :hi], vf[:hi, cols], preferred_element_type=jnp.float32
            )

        return query, jnp.concatenate([block(0, half), block(half, full)], axis=0)

    def attend(h, _):
        cols = columns_of(h)
        query, inside = inner(h)
        pair_copy(h).wait_recv()
        other = pair_in[h].astype(jnp.float32)

        @pl.when(has_prev)
        def _():
            chain_copy(h).wait_recv()

        carried = chain_in[h].astype(jnp.float32)

        @pl.when(has_next)
        def _():
            chain_out[h] = (own_weight * own[h] + other_weight * other + chain_weight * carried).astype(jnp.bfloat16)
            chain_copy(h).start()

        incoming = (inc_other * other + inc_chain * carried).astype(jnp.bfloat16)
        numerator = inside + carry_mask * jnp.dot(query, incoming, preferred_element_type=jnp.float32)
        scale = lax.rsqrt(jnp.mean(numerator * numerator, axis=1, keepdims=True) + EPSILON)
        attended[:, cols] = (numerator * scale * gain_ref[:, cols]).astype(jnp.bfloat16)
        return 0

    for g in range(parts):
        lax.fori_loop(g * heads // parts, (g + 1) * heads // parts, attend, 0)
        buckets[g] = (
            jnp.dot(chosen[...], attended[:, g * span : (g + 1) * span], preferred_element_type=jnp.float32)
            .astype(jnp.bfloat16)
            .reshape(buckets.shape[1:])
        )
        for o in order:
            tile_copy(g, o).start()
        own_copy(g).start()

    label_own.wait()
    for o in range(1, n):
        label_copy(o).wait()

    here = lax.broadcasted_iota(jnp.int32, (total.shape[0], arrived.shape[2]), 0)
    for g in range(parts):
        own_copy(g).wait()
        for o in [0] + order[::-1]:
            if o:
                tile_copy(g, o).wait_recv()
            wanted = jnp.where(here == got[o, 0:1, : arrived.shape[2]], 1.0, 0.0).astype(jnp.bfloat16)
            term = jnp.dot(wanted, arrived[g, o], preferred_element_type=jnp.float32)
            if o:
                total[...] += term
            else:
                total[...] = term
        placed[:, g * span : (g + 1) * span] = total[...].astype(jnp.bfloat16)

    def product(i, j):
        return jnp.dot(
            placed[...], weight[i, :, j * STEP : (j + 1) * STEP], preferred_element_type=jnp.float32
        )

    load(0).wait()
    for j in range(steps):
        s1[j] = product(0, j).astype(jnp.bfloat16)
        move(s1, r1, x1s, x1r, j, sib).start()
    load(1).wait()
    for j in range(steps):
        part = product(1, j)
        move(s1, r1, x1s, x1r, j, sib).wait_recv()
        s2[j] = (part.astype(jnp.bfloat16).astype(jnp.float32) + r1[j].astype(jnp.float32)).astype(jnp.bfloat16)
        move(s2, r2, x2s, x2r, j, far).start()
    load(2).wait()
    for j in range(steps):
        s3[j] = product(2, j).astype(jnp.bfloat16)
        move(s3, r3, x3s, x3r, j, sib).start()
    load(3).wait()
    for j in range(steps):
        keep[j] = product(3, j).astype(jnp.bfloat16).astype(jnp.float32)
    for j in range(steps):
        move(s3, r3, x3s, x3r, j, sib).wait_recv()
        near = keep[j] + r3[j].astype(jnp.float32)
        move(s2, r2, x2s, x2r, j, far).wait_recv()
        out_ref[:, j * STEP : (j + 1) * STEP] = (near + r2[j].astype(jnp.float32)).astype(jnp.bfloat16)
    for g in range(parts):
        for o in order:
            tile_copy(g, o).wait_send()
    for h in range(heads):
        pair_copy(h).wait_send()

        @pl.when(has_next)
        def _():
            chain_copy(h).wait_send()

    for j in range(steps):
        move(s1, r1, x1s, x1r, j, sib).wait_send()
        move(s2, r2, x2s, x2r, j, far).wait_send()
        move(s3, r3, x3s, x3r, j, sib).wait_send()


def run_kernel(tile_counts, session_starts, queries, keys, values, gain, targets, labels, out_weight, n, groups, block):
    rows, depth = queries.shape
    full = n * block
    heads = depth // DH
    columns = out_weight.shape[1]
    width = columns // groups
    steps = width // STEP
    parts = 2
    out_rows = BAL * CH
    vmem = pl.BlockSpec(memory_space=pltpu.VMEM)
    smem = pl.BlockSpec(memory_space=pltpu.SMEM)
    dma = pltpu.SemaphoreType.DMA

    def half(*shape):
        return pltpu.VMEM(shape, jnp.bfloat16)

    def single(*shape):
        return pltpu.VMEM(shape, jnp.float32)

    return pl.pallas_call(
        functools.partial(whole_kernel, n, groups, steps, parts),
        out_shape=jax.ShapeDtypeStruct((out_rows, width), jnp.bfloat16),
        in_specs=[smem, smem, vmem, vmem, vmem, vmem, vmem, vmem, pl.BlockSpec(memory_space=pl.ANY)],
        out_specs=vmem,
        scratch_shapes=[half(full, depth)] * 2
        + [half(full, full)] * 2
        + [half(full, depth), single(heads, DH, DH)]
        + [half(heads, DH, DH)] * 4
        + [pltpu.VMEM(labels.shape, jnp.int32)]
        + [half(parts, n, block, depth // parts)] * 2
        + [single(out_rows, depth // parts), half(groups, depth, width), half(out_rows, depth)]
        + [half(steps, out_rows, STEP)] * 6
        + [single(steps, out_rows, STEP)]
        + [dma((heads,))] * 4
        + [dma((n,))] * 2
        + [dma(()), dma((groups,)), dma((parts, n)), dma((parts, n)), dma((parts,))]
        + [dma((steps,))] * 6,
        compiler_params=pltpu.CompilerParams(collective_id=0, has_side_effects=True, vmem_limit_bytes=56 << 20),
        name="layer",
    )(tile_counts, session_starts, queries, keys, values, gain, targets, labels, out_weight)


def per_device(
    queries, keys, values, out_weight, norm_gain, tile_counts, route_device, route_slot, session_starts
):
    ctx_size = lax.axis_size("ctx")
    slot_count = route_device.shape[0]
    capacity = (slot_count + ctx_size - 1) // ctx_size
    block = capacity * CH
    full = ctx_size * block
    ordinal = jnp.arange(slot_count)
    clashes = (route_device[None, :] == route_device[:, None]) & (ordinal[None, :] < ordinal[:, None])
    before = jnp.sum(clashes.astype(jnp.int32), axis=1)
    target = jnp.where(route_device >= 0, route_device * capacity + before, -1)
    chosen = jnp.arange(ctx_size * capacity)[:, None] == target[None, :]
    labels = jnp.sum(jnp.where(chosen, route_slot[None, :] + 1, 0), axis=1) - 1
    within = jnp.arange(CH, dtype=jnp.int32)
    row_targets = jnp.where(target >= 0, target * CH, -CH)[:, None] + within
    row_targets = jnp.pad(row_targets.reshape(1, slot_count * CH), ((0, 0), (0, full - slot_count * CH)), constant_values=-1)
    row_labels = jnp.where(labels >= 0, labels * CH, -CH)[:, None] + within
    row_labels = jnp.pad(row_labels.reshape(ctx_size, 1, block), ((0, 0), (0, 0), (0, 128 - block)), constant_values=-1)
    row_labels = jnp.broadcast_to(row_labels, (ctx_size, 8, 128))
    return run_kernel(
        tile_counts, session_starts, queries, keys, values, norm_gain.reshape(1, -1), row_targets, row_labels,
        out_weight, ctx_size, lax.axis_size("head"), block,
    )


def solution(mesh):
    placed = (
        P("ctx", "head"),
        P("ctx", "head"),
        P("ctx", "head"),
        P("head", None),
        P("head"),
        P(),
        P("ctx"),
        P("ctx"),
        P(),
    )
    return jax.shard_map(
        per_device, mesh=mesh, in_specs=placed, out_specs=P("ctx", "head"), check_vma=False
    )
```

time: 171 us -> 77.9 us (0.46)
  Pallas kernels: 0 us -> 72.3 us
  waiting for transfers between devices: 66 us -> 0 us
  matrix products: 23.5 us -> 0 us
  blocking collectives: 22 us -> 0 us
  between operations: 16.2 us -> 0.03 us
  other arithmetic: 16.9 us -> 1.78 us
  starting transfers between devices: 11.1 us -> 0 us
  local copies, waits for them, and re-layouts: 9.1 us -> 3.52 us
  loops' own time: 5.41 us -> 0 us
    pallas_call x0 -> x1, Pallas kernels: none -> 72.3 us  [run_kernel(): pl.pallas_call(functools.partial(whole_kernel, n, groups, steps, parts),...]
    reduce_scatter x1 -> x0, waiting for transfers between devices: 30.4 us -> none  [per_device(): lax.psum_scatter(partial_value.astype(jnp.bfloat16), 'head', scatter_dime...]
    all_to_all x2 -> x0, waiting for transfers between devices: 24 us -> none  [the longest x1 24 us: deliver(): lax.all_to_all(outgoing, 'ctx', split_axis=0, concat_axis=0, tiled=True)]
    dot_general x9 -> x0, matrix products: 23.5 us -> none  [the longest x1 7.11 us: per_device(): jnp.dot(delivered, out_weight, preferred_element_type=jnp.float32)]
    unnamed x1 -> x0, blocking collectives: 22 us -> none
    all_gather x1 -> x0, waiting for transfers between devices: 11.6 us -> none  [carried_in(): lax.all_gather(part.astype(kind), axis)]
    all_to_all x2 -> x0, starting transfers between devices: 10.8 us -> none  [the longest x1 7.28 us: deliver(): lax.all_to_all(labels, 'ctx', split_axis=0, concat_axis=0, tiled=True)]
    select_n x9 -> x2, other arithmetic: 10.3 us -> 0.69 us  [the longest x1 0.69 us: per_device(): row_targets = jnp.where(target >= 0, target * CH, -CH)[:, None] + within]
  transfers between devices with their start and end apart: 4 -> 0, of which waited for: 3 -> 0; matrix products, arithmetic and copies ran while one was open for 20% -> 0% of each run, Pallas kernels for 0% -> 0%
where the time goes in v2:
time: 77.9 us; the launch traced here: 77.6 us
  Pallas kernels  72.3 us (93%)
  local copies, waits for them, and re-layouts  3.52 us (5%)
  other arithmetic  1.78 us (2%)
    pallas_call x1, Pallas kernels, run_kernel(): pl.pallas_call(functools.partial(whole_kernel, n, groups, steps, parts),...  72.3 us
    unnamed x1, local copies, waits for them, and re-layouts  1.87 us

profile of v2, /device:TPU:0, one launch (start us, length us, event | category | flops | bytes accessed | tf_op | source)
XLA Modules:
  0.0 77.6 jit_solution(2557616610923451936)
XLA Ops:
  0.0 0.9 %convert_reduce_fusion = s32[63]{0:T(128)S(1)} fusion(s32[63]{0:T(128)} %param.15), kind=kLoop, calls=%fused_computation.3 | loop fusion | flops 19782 | bytes 504 | tf_op jit(solution)/shard_map/reduce_sum | solution.py:347
  0.9 0.7 compare_select_fusion.1
  1.6 0.1 select_reduce_fusion
  1.7 0.1 select_n.26
  1.8 0.1 add.79
  1.9 0.1 add.76
  2.0 0.1 add.77
  2.1 0.6 broadcast_in_dim.47.labels_ref
  2.7 0.1 iota_add_fusion
  2.8 0.1 add.73
  2.9 0.6 pad.8.target_ref
  3.5 72.3 %layer.1 = bf16[256,1024]{1,0:T(8,128)(2,1)} custom-call(s32[8]{0:T(128)} %counts_ref.1, s32[4]{0:T(128)} %starts_ref.1, bf16[504,1024]{1,0:T(8,128)(2,1)} %q_ref.1, bf16[504,1024]{1,0:T(8,128)(2,1)} %k_ref.1, bf16[504,1024]{1,0:T(8,128)(2,1)} %v_ref.1, f32[1,1024]{1,0:T(1,128)} %bitcast.3, s32[1,512]{1,0:T(1,128)} %pad.8.target_ref, ...), custom_call_target="tpu_custom_call" | custom-call | tf_op jit(solution)/shard_map/layer/pallas_call | solution.py:314
  75.8 1.9 %copy.11 = bf16[256,1024]{1,0:T(8,128)(2,1)} copy(bf16[256,1024]{1,0:T(8,128)(2,1)} %layer.1) | data formatting | bytes 1048576
  (4 shorter events, 0.0 us)
